TPU v7x, 32 devices: a whole 2x2x4 slice. The times are simulated.
32 devices in a mesh: rows: 8 (over z, x), vocab: 4 (over y, core).
Axes of the slice: x: 2, y: 2, z: 4, core: 2. Of those that a mesh axis runs over, the one named last changes fastest.
Arguments:
- hidden_rows: bfloat16 [128, 8192], P('vocab', 'rows'), may hold values from -24 to 24
- row_states: int32 [128], P('vocab'), may hold values from 0 to 511
- head_weight: bfloat16 [8192, 152064], P(None, ('rows', 'vocab')), may hold values from -2 to 2
- grammar_table: int32 [512, 152064], P(None, ('rows', 'vocab')), may hold values from 0 to 1, as said below
Outputs:
- log_probs: float32 [128, 152064], P(None, ('rows', 'vocab'))
- normalizer: float32 [128], replicated
Inputs may be any that keep to these rules, and one draw needn't show every extreme that they name: `grammar_table`: every state allows the tokens 0 to 31.
All inputs are finite; a program needn't handle non-finite values.
Results may differ from a plain program's by a relative error of at most 0.0003.
Values may be sent and summed in bfloat16 or wider, within the bound.
No kernel may reach another device: no remote copies, remote signals or barrier semaphores. Data moves between devices by JAX's collectives and lax.ppermute only.
A program may use at most 128 MiB of HBM per device.

v0:
```python
import functools

import jax
import jax.numpy as jnp
from jax import lax
from jax.experimental import pallas as pl
from jax.experimental.pallas import tpu as pltpu
from jax.sharding import PartitionSpec as P

lowest = -1e30
reachable = -1e29
slots = 4


def ring_order(size):
    return list(range(0, size, 2)) + list(range(1, size, 2))[::-1]


def swap(x, axis, size, distance):
    return lax.ppermute(x, axis, [(i, i ^ distance) for i in range(size)])


def row_tile(columns):
    fits = [t for t in range(16, 529, 16) if columns % t == 0]
    return max(fits) if fits else columns


def ring_place(offset, count):
    here = lax.axis_index("rows")
    half = here // 2
    spot = jnp.where(here % 2 == 0, half, count - 1 - half)
    spot = lax.rem(spot + offset + count, count)
    return jnp.where(spot < count // 2, 2 * spot, 2 * (count - 1 - spot) + 1)


def stage_kernel(plan, *refs):
    rows_count, block, depth, columns, all_rows = plan["sizes"]
    refs = list(refs)
    take = lambda n: [refs.pop(0) for _ in range(n)]
    (weight,) = take(1)
    if plan["load_table"]:
        (table_in,) = take(1)
    else:
        take(1)
    if plan["first"]:
        states, table = take(plan["vocab_count"]), take(1)[0]
    elif plan["compute"]:
        take(1)
    chunks = [(slot, take(2)) for slot in plan["compute"]]
    (held,) = take(1)
    acc = take(1)[0] if plan["compute"] else None
    lse = take(1)[0] if plan["last"] else None
    table_out = take(1)[0] if plan["load_table"] else None
    hidden, turned, marks, sems = take(4)

    tile = row_tile(columns)
    tiles = columns // tile
    copies = []
    for offset, slot in plan["load"]:
        at = pl.multiple_of(ring_place(offset, rows_count) * depth, depth)
        for t in range(tiles):
            span = pl.ds(t * tile, tile)
            copies.append((weight.at[span, pl.ds(at, depth)], held.at[slot, span, :]))
    if plan["load_table"]:
        for t in range(tiles):
            span = pl.ds(t * tile, tile)
            copies.append((table_in.at[span, :], table_out.at[span, :]))
    copies = [pltpu.make_async_copy(a, b, sems.at[n]) for n, (a, b) in enumerate(copies)]
    for copy in copies:
        copy.start()

    if plan["compute"]:
        vocab_at = lax.axis_index("vocab")
        for c, (_, pieces) in enumerate(chunks):
            for other, ref in enumerate(pieces):
                for j in range(ref.shape[0] // block):
                    owner = vocab_at ^ (2 * j + other)
                    at = pl.multiple_of(owner * block, block)
                    hidden[pl.ds(at, block), :] = ref[j * block : (j + 1) * block, :]
            turned[c] = hidden[...].astype(jnp.float32).T.astype(jnp.bfloat16)
        if plan["first"]:
            state_count = table.shape[1]
            state = lax.broadcasted_iota(jnp.int32, (state_count, all_rows), 0)
            owner = lax.broadcasted_iota(jnp.int32, (1, all_rows), 1) // block
            wanted = jnp.zeros((1, all_rows), jnp.int32)
            for d, part in enumerate(states):
                wanted = jnp.where(owner == (vocab_at ^ d), jnp.tile(part[...], (1, all_rows // block)), wanted)
            marks[...] = (state == wanted).astype(jnp.float32).astype(jnp.bfloat16)

        def work(t, carry):
            span = pl.ds(pl.multiple_of(t * tile, tile), tile) if tiles > 1 else slice(None)
            if plan["first"]:
                rules = table[span, :].astype(jnp.float32).astype(jnp.bfloat16)
                allowed = jnp.dot(rules, marks[...], preferred_element_type=jnp.float32) > 0.5
                total = jnp.where(allowed, 0.0, lowest)
            else:
                total = acc[span, :]
            for c, (slot, _) in enumerate(chunks):
                total += jnp.dot(held[slot, span, :], turned[c], preferred_element_type=jnp.float32)
            acc[span, :] = total
            if plan["last"]:
                peak, exps = carry
                new_peak = jnp.maximum(peak, jnp.max(total, axis=0, keepdims=True))
                terms = jnp.where(total > reachable, jnp.exp(total - new_peak), 0.0)
                exps = exps * jnp.exp(peak - new_peak) + jnp.sum(terms, axis=0, keepdims=True)
                return new_peak, exps
            return carry

        start = ()
        if plan["last"]:
            start = (jnp.full((1, all_rows), lowest, jnp.float32), jnp.zeros((1, all_rows), jnp.float32))
        done = lax.fori_loop(0, tiles, work, start, unroll=True)
        if plan["last"]:
            peak, exps = done
            lse[...] = jnp.where(exps > 0.0, peak + jnp.log(exps), lowest)

    for copy in copies:
        copy.wait()


def stage(plan, weight, table_in, states, table, held, acc, chunks):
    rows_count, block, depth, columns, all_rows = plan["sizes"]
    vmem = pl.BlockSpec(memory_space=pltpu.VMEM)
    keep = lambda x: pltpu.with_memory_space_constraint(x, pltpu.VMEM)
    args, specs, out, alias = [weight], [pl.BlockSpec(memory_space=pl.ANY)], [], {}
    state_count = table_in.shape[1]
    if plan["load_table"]:
        args.append(pltpu.with_memory_space_constraint(table_in, pltpu.HBM))
        specs.append(pl.BlockSpec(memory_space=pltpu.HBM))
    else:
        alias[len(args)] = 0
        args.append(keep(held))
        specs.append(vmem)
    if plan["first"]:
        args += [*states, keep(table)]
        specs += [vmem] * (len(states) + 1)
    elif plan["compute"]:
        alias[len(args)] = 1
        args.append(keep(acc))
        specs.append(vmem)
    args += [p for pieces in chunks for p in pieces]
    specs += [vmem] * sum(len(pieces) for pieces in chunks)
    out.append(pltpu.VMEM((slots, columns, depth), jnp.bfloat16))
    if plan["compute"]:
        out.append(pltpu.VMEM((columns, all_rows), jnp.float32))
    if plan["last"]:
        out.append(jax.ShapeDtypeStruct((1, all_rows), jnp.float32))
    if plan["load_table"]:
        out.append(pltpu.VMEM((columns, state_count), jnp.int32))
    tiles = columns // row_tile(columns)
    moved = 2 * columns * depth * len(plan["load"]) + 4 * columns * state_count * plan["load_table"]
    return pl.pallas_call(
        functools.partial(stage_kernel, plan),
        in_specs=specs,
        out_shape=out,
        out_specs=[vmem] * len(out),
        input_output_aliases=alias,
        scratch_shapes=[
            pltpu.VMEM((all_rows, depth), jnp.bfloat16),
            pltpu.VMEM((max(1, len(plan["compute"])), depth, all_rows), jnp.bfloat16),
            pltpu.VMEM((state_count, all_rows), jnp.bfloat16),
            pltpu.SemaphoreType.DMA((max(1, tiles * (len(plan["load"]) + plan["load_table"])),)),
        ],
        compiler_params=pltpu.CompilerParams(vmem_limit_bytes=5 * 2**20),
        cost_estimate=pl.CostEstimate(
            flops=2 * all_rows * depth * columns * len(plan["compute"]),
            bytes_accessed=moved,
            transcendentals=all_rows * columns * plan["last"],
        ),
    )(*args)


def join_kernel(*refs):
    size = refs[0].shape[0]
    for i, ref in enumerate(refs[:-1]):
        refs[-1][i * size : (i + 1) * size, :] = ref[...]


def join(parts):
    rows, width = parts[0].shape
    return pl.pallas_call(
        join_kernel,
        in_specs=[pl.BlockSpec(memory_space=pltpu.VMEM)] * len(parts),
        out_specs=pl.BlockSpec(memory_space=pltpu.VMEM),
        out_shape=jax.ShapeDtypeStruct((rows * len(parts), width), parts[0].dtype),
        compiler_params=pltpu.CompilerParams(vmem_limit_bytes=2 * 2**20),
    )(*parts)


def local(rows_count, vocab_count, hidden_rows, row_states, head_weight, grammar_table):
    block, depth = hidden_rows.shape
    columns = head_weight.shape[1]
    half = vocab_count // 2
    all_rows = block * vocab_count
    weight, table_in = head_weight.T, grammar_table.T

    row_states = row_states.reshape(1, block)
    states = [row_states] + [swap(row_states, "vocab", vocab_count, d) for d in range(1, vocab_count)]
    own = [hidden_rows] + [swap(hidden_rows, "vocab", vocab_count, 2 * d) for d in range(1, half)]
    plan = dict(
        vocab_count=vocab_count,
        sizes=(rows_count, block, depth, columns, all_rows),
        load=[(0, 0)],
        compute=[],
        load_table=True,
        first=False,
        last=False,
    )
    held, table = stage(plan, weight, table_in, states, None, None, None, [])
    own, states, held, table = lax.optimization_barrier((own, states, held, table))
    own = join(own)

    order = ring_order(rows_count)
    ahead = [(order[i], order[(i + 1) % rows_count]) for i in range(rows_count)]
    back = [(b, a) for a, b in ahead]
    last_hop = rows_count // 2
    acc, load, used = None, plan["load"], 1
    arrived = [(0, own)]
    up = down = own
    for j in range(1, last_hop + 2):
        coming = []
        if j < last_hop:
            coming = [(-j, lax.ppermute(up, "rows", ahead)), (j, lax.ppermute(down, "rows", back))]
        elif j == last_hop:
            coming = [(j, lax.ppermute(up, "rows", ahead))]
        compute = [slot for _, slot in load]
        chunks = [[piece, swap(piece, "vocab", vocab_count, 1)] for _, piece in arrived]
        load = [(offset, (used + i) % slots) for i, (offset, _) in enumerate(coming)]
        used += len(load)
        plan = dict(
            vocab_count=vocab_count,
            sizes=(rows_count, block, depth, columns, all_rows),
            load=load,
            compute=compute,
            load_table=False,
            first=j == 1,
            last=j > last_hop,
        )
        res = list(stage(plan, weight, table_in, states, table, held, acc, chunks))
        held, acc = res[:2]
        if plan["last"]:
            lse = res[2]
        else:
            pieces, held, acc = lax.optimization_barrier(([p for _, p in coming], held, acc))
            arrived = [(offset, p) for (offset, _), p in zip(coming, pieces)]
            up, down = pieces[0], pieces[-1]

    count = rows_count * vocab_count
    sent = jnp.broadcast_to(lse[None], (count, 1, all_rows))
    parts = lax.all_to_all(sent, ("rows", "vocab"), 0, 0, tiled=True)
    top = jnp.max(parts, axis=0)
    lse = top + jnp.log(jnp.sum(jnp.exp(parts - top), axis=0))
    log_probs = jnp.where(acc > reachable, acc - lse, 0.0)
    return log_probs.T, lse.reshape(all_rows)


def solution(mesh):
    placed = (
        P("vocab", "rows"),
        P("vocab"),
        P(None, ("rows", "vocab")),
        P(None, ("rows", "vocab")),
    )
    return jax.shard_map(
        functools.partial(local, mesh.shape["rows"], mesh.shape["vocab"]),
        mesh=mesh,
        in_specs=placed,
        out_specs=(P(None, ("rows", "vocab")), P()),
        check_vma=False,
    )
```

profile of v0, /device:TPU:0, one launch (start us, length us, event | category | flops | bytes accessed | tf_op | source)
XLA Modules:
  0.0 67.5 jit_solution(17636416387407467873)
XLA Ops:
  0.6 3.0 %collective-permute-start = (bf16[32,1024]{1,0:T(8,128)(2,1)}, bf16[32,1024]{1,0:T(8,128)(2,1)S(1)}, u32[]{:S(2)}, u32[]{:S(2)}) collective-permute-start(bf16[32,1024]{1,0:T(8,128)(2,1)} %refs_0_), channel_id=1, source_target_pairs={{0,2},{1,3},{2,0},{3,1},{4,6},{5,7},{6,4},{7,5},{8,10},{9,11},{10,... | collective-permute-start | bytes 196616 | tf_op jit(solution)/shard_map/ppermute | solution.py:20
  3.7 0.0 collective-permute-start.3
  3.7 1.2 %collective-permute-start.2 = (s32[1,32]{1,0:T(1,128)}, s32[1,32]{1,0:T(1,128)S(1)}, u32[]{:S(2)}, u32[]{:S(2)}) collective-permute-start(s32[1,32]{1,0:T(1,128)} %bitcast.9), channel_id=1, source_target_pairs={{0,2},{1,3},{2,0},{3,1},{4,6},{5,7},{6,4},{7,5},{8,10},{9,11},{10,... | collective-permute-start | bytes 392 | tf_op jit(solution)/shard_map/ppermute | solution.py:20
  4.8 0.7 %collective-permute-start.1 = (s32[1,32]{1,0:T(1,128)}, s32[1,32]{1,0:T(1,128)S(1)}, u32[]{:S(2)}, u32[]{:S(2)}) collective-permute-start(s32[1,32]{1,0:T(1,128)} %bitcast.10), channel_id=1, source_target_pairs={{0,1},{1,0},{2,3},{3,2},{4,5},{5,4},{6,7},{7,6},{8,9},{9,8},{10,11... | collective-permute-start | bytes 392 | tf_op jit(solution)/shard_map/ppermute | solution.py:20
  5.5 6.8 %shard_map.59 = (bf16[4,4752,1024]{2,1,0:T(8,128)(2,1)S(1)}, s32[4752,512]{1,0:T(8,128)S(1)}) custom-call(bf16[4752,8192]{1,0:T(8,128)(2,1)} %bitcast.refs_0_, s32[4752,512]{1,0:T(8,128)} %bitcast.12), custom_call_target="tpu_custom_call" | custom-call | bytes 19464192 | tf_op jit(solution)/shard_map/pallas_call | solution.py:152
  12.3 0.0 collective-permute-done.3.refs_5_
  12.3 0.0 collective-permute-done.2.refs_4_
  12.3 0.0 collective-permute-done.1.refs_3_
  12.3 0.0 collective-permute-done.refs_1_
  12.4 0.1 collective-permute-start.6
  12.5 1.5 %collective-permute-start.5 = (bf16[64,1024]{1,0:T(8,128)(2,1)S(1)}, bf16[64,1024]{1,0:T(8,128)(2,1)S(1)}, u32[]{:S(2)}, u32[]{:S(2)}) collective-permute-start(bf16[64,1024]{1,0:T(8,128)(2,1)S(1)} %shard_map.60.refs_7_), channel_id=1, source_target_pairs={{8,0},{16,8},{24,16},{28,24},{20,28},{12,20},{4,12},{0,4},{9,1},{1... | collective-permute-start | bytes 393224 | tf_op jit(solution)/shard_map/ppermute | solution.py:223
  14.0 0.5 collective-permute-start.4
  14.5 0.0 collective-permute-done.6.refs_8_
  14.6 0.7 copy-done.2
  15.2 7.8 %shard_map.61 = (bf16[4,4752,1024]{2,1,0:T(8,128)(2,1)S(1)}, f32[4752,128]{1,0:T(8,128)S(1)}) custom-call(bf16[4752,8192]{1,0:T(8,128)(2,1)} %bitcast.refs_0_, bf16[4,4752,1024]{2,1,0:T(8,128)(2,1)S(1)} %get-tuple-element.41.refs_1_, s32[1,32]{1,0:T(1,128)S(1)} %bitcast.11, ...), custom_call_target="tpu_custom_call", output_to_operand_aliasing={{0}: (1, {})} | custom-call | flops 1245708288 | bytes 19464192 | tf_op jit(solution)/shard_map/pallas_call | solution.py:152
  23.0 0.0 collective-permute-done.5.refs_5_
  23.0 0.0 collective-permute-done.4.refs_3_
  23.0 0.1 collective-permute-start.9
  23.1 0.5 collective-permute-start.10
  23.6 1.6 %collective-permute-start.7 = (bf16[64,1024]{1,0:T(8,128)(2,1)S(1)}, bf16[64,1024]{1,0:T(8,128)(2,1)S(1)}, u32[]{:S(2)}, u32[]{:S(2)}) collective-permute-start(bf16[64,1024]{1,0:T(8,128)(2,1)S(1)} %collective-permute-done.4.refs_3_), channel_id=1, source_target_pairs={{0,8},{8,16},{16,24},{24,28},{28,20},{20,12},{12,4},{4,0},{1,9},{9... | collective-permute-start | bytes 393224 | tf_op jit(solution)/shard_map/ppermute | solution.py:223
  25.2 0.4 collective-permute-start.8
  25.6 0.0 collective-permute-done.9.refs_4_
  25.6 0.0 collective-permute-done.10.refs_6_
  25.6 6.9 %shard_map.62 = (bf16[4,4752,1024]{2,1,0:T(8,128)(2,1)S(1)}, f32[4752,128]{1,0:T(8,128)S(1)}) custom-call(bf16[4752,8192]{1,0:T(8,128)(2,1)} %bitcast.refs_0_, bf16[4,4752,1024]{2,1,0:T(8,128)(2,1)S(1)} %get-tuple-element.51.refs_1_, f32[4752,128]{1,0:T(8,128)S(1)} %get-tuple-element.52.refs_2_, ...), custom_call_target="tpu_custom_call", output_to_operand_aliasing={{0}: (1, {}), {1}: (2, {})} | custom-call | flops 2491416576 | bytes 19464192 | tf_op jit(solution)/shard_map/pallas_call | solution.py:152
  32.5 0.0 collective-permute-done.7.refs_3_
  32.5 0.0 collective-permute-done.8.refs_5_
  32.5 0.1 collective-permute-start.13
  32.6 0.5 collective-permute-start.14
  33.1 1.6 %collective-permute-start.11 = (bf16[64,1024]{1,0:T(8,128)(2,1)S(1)}, bf16[64,1024]{1,0:T(8,128)(2,1)S(1)}, u32[]{:S(2)}, u32[]{:S(2)}) collective-permute-start(bf16[64,1024]{1,0:T(8,128)(2,1)S(1)} %collective-permute-done.7.refs_3_), channel_id=1, source_target_pairs={{0,8},{8,16},{16,24},{24,28},{28,20},{20,12},{12,4},{4,0},{1,9},{9... | collective-permute-start | bytes 393224 | tf_op jit(solution)/shard_map/ppermute | solution.py:223
  34.7 0.5 collective-permute-start.12
  35.1 0.0 collective-permute-done.13.refs_4_
  35.1 0.0 collective-permute-done.14.refs_6_
  35.1 6.9 %shard_map.63 = (bf16[4,4752,1024]{2,1,0:T(8,128)(2,1)S(1)}, f32[4752,128]{1,0:T(8,128)S(1)}) custom-call(bf16[4752,8192]{1,0:T(8,128)(2,1)} %bitcast.refs_0_, bf16[4,4752,1024]{2,1,0:T(8,128)(2,1)S(1)} %get-tuple-element.57.refs_1_, f32[4752,128]{1,0:T(8,128)S(1)} %get-tuple-element.58.refs_2_, ...), custom_call_target="tpu_custom_call", output_to_operand_aliasing={{0}: (1, {}), {1}: (2, {})} | custom-call | flops 2491416576 | bytes 19464192 | tf_op jit(solution)/shard_map/pallas_call | solution.py:152
  42.0 0.0 collective-permute-done.11.refs_3_
  42.0 0.0 collective-permute-done.12.refs_5_
  42.0 0.1 collective-permute-start.17
  42.1 0.5 collective-permute-start.16
  42.6 1.6 %collective-permute-start.15 = (bf16[64,1024]{1,0:T(8,128)(2,1)S(1)}, bf16[64,1024]{1,0:T(8,128)(2,1)S(1)}, u32[]{:S(2)}, u32[]{:S(2)}) collective-permute-start(bf16[64,1024]{1,0:T(8,128)(2,1)S(1)} %collective-permute-done.11.refs_3_), channel_id=1, source_target_pairs={{0,8},{8,16},{16,24},{24,28},{28,20},{20,12},{12,4},{4,0},{1,9},{9... | collective-permute-start | bytes 393224 | tf_op jit(solution)/shard_map/ppermute | solution.py:225
  44.2 0.0 collective-permute-done.17.refs_6_
  44.2 0.0 collective-permute-done.16.refs_4_
  44.2 5.5 %shard_map.64 = (bf16[4,4752,1024]{2,1,0:T(8,128)(2,1)S(1)}, f32[4752,128]{1,0:T(8,128)S(1)}) custom-call(bf16[4752,8192]{1,0:T(8,128)(2,1)} %bitcast.refs_0_, bf16[4,4752,1024]{2,1,0:T(8,128)(2,1)S(1)} %get-tuple-element.62.refs_1_, f32[4752,128]{1,0:T(8,128)S(1)} %get-tuple-element.63.refs_2_, ...), custom_call_target="tpu_custom_call", output_to_operand_aliasing={{0}: (1, {}), {1}: (2, {})} | custom-call | flops 2491416576 | bytes 9732096 | tf_op jit(solution)/shard_map/pallas_call | solution.py:152
  49.7 0.0 collective-permute-done.15.refs_3_
  49.7 0.1 collective-permute-start.18
  49.8 1.3 %collective-permute-done.18.refs_4_ = bf16[64,1024]{1,0:T(8,128)(2,1)S(1)} collective-permute-done((bf16[64,1024]{1,0:T(8,128)(2,1)S(1)}, bf16[64,1024]{1,0:T(8,128)(2,1)S(1)}, u32[]{:S(2)}, u32[]{:S(2)}) %collective-permute-start.18) | collective-permute-done | bytes 131104 | tf_op jit(solution)/shard_map/ppermute | solution.py:20
  51.1 3.3 %shard_map.65 = (bf16[4,4752,1024]{2,1,0:T(8,128)(2,1)S(1)}, f32[4752,128]{1,0:T(8,128)S(1)}, f32[1,128]{1,0:T(1,128)S(1)}) custom-call(bf16[4752,8192]{1,0:T(8,128)(2,1)} %bitcast.refs_0_, bf16[4,4752,1024]{2,1,0:T(8,128)(2,1)S(1)} %get-tuple-element.67.refs_1_, ...), custom_call_target="tpu_custom_call", output_to_operand_aliasing={{0}: (1, {}), {1}: (2, {})} | custom-call | flops 1245708288 | tf_op jit(solution)/shard_map/pallas_call | solution.py:152
  54.4 11.4 %all_to_all.5 = f32[32,1,128]{2,1,0:T(1,128)S(1)} all-to-all(f32[32,1,128]{2,1,0:T(1,128)S(1)} %broadcast_in_dim.14), channel_id=1, replica_groups=mesh['rows'=8,'vocab'=4] {'rows','vocab'}, dimensions={0} | all-to-all | bytes 32768 | tf_op jit(solution)/shard_map/all_to_all | solution.py:250
  65.8 0.0 copy-start.3
  65.8 1.7 %select_bitcast_fusion = f32[128,4752]{0,1:T(8,128)} fusion(f32[4752,128]{1,0:T(8,128)S(1)} %get-tuple-element.70, f32[128]{0:T(128)S(1)} %log_add_fusion), kind=kLoop, calls=%fused_computation | loop fusion | flops 1824768 | bytes 4866560 | tf_op jit(solution)/shard_map/transpose | solution.py:254
  (11 shorter events, 0.1 us)
Async XLA Ops:
  0.6 11.7 %collective-permute-start = (bf16[32,1024]{1,0:T(8,128)(2,1)}, bf16[32,1024]{1,0:T(8,128)(2,1)S(1)}, u32[]{:S(2)}, u32[]{:S(2)}) collective-permute-start(bf16[32,1024]{1,0:T(8,128)(2,1)} %refs_0_), channel_id=1, source_target_pairs={{0,2},{1,3},{2,0},{3,1},{4,6},{5,7},{6,4},{7,5},{8,10},{9,11},{10,... | collective-permute-start | bytes 196616 | tf_op jit(solution)/shard_map/ppermute | solution.py:20
  3.7 8.7 %collective-permute-start.3 = (s32[1,32]{1,0:T(1,128)}, s32[1,32]{1,0:T(1,128)S(1)}, u32[]{:S(2)}, u32[]{:S(2)}) collective-permute-start(s32[1,32]{1,0:T(1,128)} %bitcast.8), channel_id=1, source_target_pairs={{0,3},{1,2},{2,1},{3,0},{4,7},{5,6},{6,5},{7,4},{8,11},{9,10},{10,... | collective-permute-start | bytes 392 | tf_op jit(solution)/shard_map/ppermute | solution.py:20
  3.7 8.7 %collective-permute-start.2 = (s32[1,32]{1,0:T(1,128)}, s32[1,32]{1,0:T(1,128)S(1)}, u32[]{:S(2)}, u32[]{:S(2)}) collective-permute-start(s32[1,32]{1,0:T(1,128)} %bitcast.9), channel_id=1, source_target_pairs={{0,2},{1,3},{2,0},{3,1},{4,6},{5,7},{6,4},{7,5},{8,10},{9,11},{10,... | collective-permute-start | bytes 392 | tf_op jit(solution)/shard_map/ppermute | solution.py:20
  4.8 7.5 %collective-permute-start.1 = (s32[1,32]{1,0:T(1,128)}, s32[1,32]{1,0:T(1,128)S(1)}, u32[]{:S(2)}, u32[]{:S(2)}) collective-permute-start(s32[1,32]{1,0:T(1,128)} %bitcast.10), channel_id=1, source_target_pairs={{0,1},{1,0},{2,3},{3,2},{4,5},{5,4},{6,7},{7,6},{8,9},{9,8},{10,11... | collective-permute-start | bytes 392 | tf_op jit(solution)/shard_map/ppermute | solution.py:20
  5.5 6.8 %copy-start = (bf16[32,1024]{1,0:T(8,128)(2,1)S(1)}, bf16[32,1024]{1,0:T(8,128)(2,1)}, u32[]{:S(2)}) copy-start(bf16[32,1024]{1,0:T(8,128)(2,1)} %refs_0_) | copy-start | bytes 196612
  5.5 9.7 %copy-start.1 = (s32[32]{0:T(128)S(1)}, s32[32]{0:T(128)}, u32[]{:S(2)}) copy-start(s32[32]{0:T(128)} %param.5) | copy-start | bytes 388
  12.4 2.2 %collective-permute-start.6 = (bf16[64,1024]{1,0:T(8,128)(2,1)S(1)}, bf16[64,1024]{1,0:T(8,128)(2,1)S(1)}, u32[]{:S(2)}, u32[]{:S(2)}) collective-permute-start(bf16[64,1024]{1,0:T(8,128)(2,1)S(1)} %shard_map.60.refs_7_), channel_id=1, source_target_pairs={{0,1},{1,0},{2,3},{3,2},{4,5},{5,4},{6,7},{7,6},{8,9},{9,8},{10,11... | collective-permute-start | bytes 393224 | tf_op jit(solution)/shard_map/ppermute | solution.py:20
  12.5 10.5 %collective-permute-start.5 = (bf16[64,1024]{1,0:T(8,128)(2,1)S(1)}, bf16[64,1024]{1,0:T(8,128)(2,1)S(1)}, u32[]{:S(2)}, u32[]{:S(2)}) collective-permute-start(bf16[64,1024]{1,0:T(8,128)(2,1)S(1)} %shard_map.60.refs_7_), channel_id=1, source_target_pairs={{8,0},{16,8},{24,16},{28,24},{20,28},{12,20},{4,12},{0,4},{9,1},{1... | collective-permute-start | bytes 393224 | tf_op jit(solution)/shard_map/ppermute | solution.py:223
  14.0 9.0 %collective-permute-start.4 = (bf16[64,1024]{1,0:T(8,128)(2,1)S(1)}, bf16[64,1024]{1,0:T(8,128)(2,1)S(1)}, u32[]{:S(2)}, u32[]{:S(2)}) collective-permute-start(bf16[64,1024]{1,0:T(8,128)(2,1)S(1)} %shard_map.60.refs_7_), channel_id=1, source_target_pairs={{0,8},{8,16},{16,24},{24,28},{28,20},{20,12},{12,4},{4,0},{1,9},{9... | collective-permute-start | bytes 393224 | tf_op jit(solution)/shard_map/ppermute | solution.py:223
  14.5 0.7 copy-start.2
  23.0 2.6 %collective-permute-start.9 = (bf16[64,1024]{1,0:T(8,128)(2,1)S(1)}, bf16[64,1024]{1,0:T(8,128)(2,1)S(1)}, u32[]{:S(2)}, u32[]{:S(2)}) collective-permute-start(bf16[64,1024]{1,0:T(8,128)(2,1)S(1)} %collective-permute-done.4.refs_3_), channel_id=1, source_target_pairs={{0,1},{1,0},{2,3},{3,2},{4,5},{5,4},{6,7},{7,6},{8,9},{9,8},{10,11... | collective-permute-start | bytes 393224 | tf_op jit(solution)/shard_map/ppermute | solution.py:20
  23.1 2.5 %collective-permute-start.10 = (bf16[64,1024]{1,0:T(8,128)(2,1)S(1)}, bf16[64,1024]{1,0:T(8,128)(2,1)S(1)}, u32[]{:S(2)}, u32[]{:S(2)}) collective-permute-start(bf16[64,1024]{1,0:T(8,128)(2,1)S(1)} %collective-permute-done.5.refs_5_), channel_id=1, source_target_pairs={{0,1},{1,0},{2,3},{3,2},{4,5},{5,4},{6,7},{7,6},{8,9},{9,8},{10,11... | collective-permute-start | bytes 393224 | tf_op jit(solution)/shard_map/ppermute | solution.py:20
  23.6 8.9 %collective-permute-start.7 = (bf16[64,1024]{1,0:T(8,128)(2,1)S(1)}, bf16[64,1024]{1,0:T(8,128)(2,1)S(1)}, u32[]{:S(2)}, u32[]{:S(2)}) collective-permute-start(bf16[64,1024]{1,0:T(8,128)(2,1)S(1)} %collective-permute-done.4.refs_3_), channel_id=1, source_target_pairs={{0,8},{8,16},{16,24},{24,28},{28,20},{20,12},{12,4},{4,0},{1,9},{9... | collective-permute-start | bytes 393224 | tf_op jit(solution)/shard_map/ppermute | solution.py:223
  25.2 7.3 %collective-permute-start.8 = (bf16[64,1024]{1,0:T(8,128)(2,1)S(1)}, bf16[64,1024]{1,0:T(8,128)(2,1)S(1)}, u32[]{:S(2)}, u32[]{:S(2)}) collective-permute-start(bf16[64,1024]{1,0:T(8,128)(2,1)S(1)} %collective-permute-done.5.refs_5_), channel_id=1, source_target_pairs={{8,0},{16,8},{24,16},{28,24},{20,28},{12,20},{4,12},{0,4},{9,1},{1... | collective-permute-start | bytes 393224 | tf_op jit(solution)/shard_map/ppermute | solution.py:223
  32.5 2.6 %collective-permute-start.13 = (bf16[64,1024]{1,0:T(8,128)(2,1)S(1)}, bf16[64,1024]{1,0:T(8,128)(2,1)S(1)}, u32[]{:S(2)}, u32[]{:S(2)}) collective-permute-start(bf16[64,1024]{1,0:T(8,128)(2,1)S(1)} %collective-permute-done.7.refs_3_), channel_id=1, source_target_pairs={{0,1},{1,0},{2,3},{3,2},{4,5},{5,4},{6,7},{7,6},{8,9},{9,8},{10,11... | collective-permute-start | bytes 393224 | tf_op jit(solution)/shard_map/ppermute | solution.py:20
  32.6 2.5 %collective-permute-start.14 = (bf16[64,1024]{1,0:T(8,128)(2,1)S(1)}, bf16[64,1024]{1,0:T(8,128)(2,1)S(1)}, u32[]{:S(2)}, u32[]{:S(2)}) collective-permute-start(bf16[64,1024]{1,0:T(8,128)(2,1)S(1)} %collective-permute-done.8.refs_5_), channel_id=1, source_target_pairs={{0,1},{1,0},{2,3},{3,2},{4,5},{5,4},{6,7},{7,6},{8,9},{9,8},{10,11... | collective-permute-start | bytes 393224 | tf_op jit(solution)/shard_map/ppermute | solution.py:20
  33.1 8.9 %collective-permute-start.11 = (bf16[64,1024]{1,0:T(8,128)(2,1)S(1)}, bf16[64,1024]{1,0:T(8,128)(2,1)S(1)}, u32[]{:S(2)}, u32[]{:S(2)}) collective-permute-start(bf16[64,1024]{1,0:T(8,128)(2,1)S(1)} %collective-permute-done.7.refs_3_), channel_id=1, source_target_pairs={{0,8},{8,16},{16,24},{24,28},{28,20},{20,12},{12,4},{4,0},{1,9},{9... | collective-permute-start | bytes 393224 | tf_op jit(solution)/shard_map/ppermute | solution.py:223
  34.7 7.3 %collective-permute-start.12 = (bf16[64,1024]{1,0:T(8,128)(2,1)S(1)}, bf16[64,1024]{1,0:T(8,128)(2,1)S(1)}, u32[]{:S(2)}, u32[]{:S(2)}) collective-permute-start(bf16[64,1024]{1,0:T(8,128)(2,1)S(1)} %collective-permute-done.8.refs_5_), channel_id=1, source_target_pairs={{8,0},{16,8},{24,16},{28,24},{20,28},{12,20},{4,12},{0,4},{9,1},{1... | collective-permute-start | bytes 393224 | tf_op jit(solution)/shard_map/ppermute | solution.py:223
  42.0 2.2 %collective-permute-start.17 = (bf16[64,1024]{1,0:T(8,128)(2,1)S(1)}, bf16[64,1024]{1,0:T(8,128)(2,1)S(1)}, u32[]{:S(2)}, u32[]{:S(2)}) collective-permute-start(bf16[64,1024]{1,0:T(8,128)(2,1)S(1)} %collective-permute-done.12.refs_5_), channel_id=1, source_target_pairs={{0,1},{1,0},{2,3},{3,2},{4,5},{5,4},{6,7},{7,6},{8,9},{9,8},{10,11... | collective-permute-start | bytes 393224 | tf_op jit(solution)/shard_map/ppermute | solution.py:20
  42.1 2.1 %collective-permute-start.16 = (bf16[64,1024]{1,0:T(8,128)(2,1)S(1)}, bf16[64,1024]{1,0:T(8,128)(2,1)S(1)}, u32[]{:S(2)}, u32[]{:S(2)}) collective-permute-start(bf16[64,1024]{1,0:T(8,128)(2,1)S(1)} %collective-permute-done.11.refs_3_), channel_id=1, source_target_pairs={{0,1},{1,0},{2,3},{3,2},{4,5},{5,4},{6,7},{7,6},{8,9},{9,8},{10,11... | collective-permute-start | bytes 393224 | tf_op jit(solution)/shard_map/ppermute | solution.py:20
  42.6 7.1 %collective-permute-start.15 = (bf16[64,1024]{1,0:T(8,128)(2,1)S(1)}, bf16[64,1024]{1,0:T(8,128)(2,1)S(1)}, u32[]{:S(2)}, u32[]{:S(2)}) collective-permute-start(bf16[64,1024]{1,0:T(8,128)(2,1)S(1)} %collective-permute-done.11.refs_3_), channel_id=1, source_target_pairs={{0,8},{8,16},{16,24},{24,28},{28,20},{20,12},{12,4},{4,0},{1,9},{9... | collective-permute-start | bytes 393224 | tf_op jit(solution)/shard_map/ppermute | solution.py:225
  49.7 1.4 %collective-permute-start.18 = (bf16[64,1024]{1,0:T(8,128)(2,1)S(1)}, bf16[64,1024]{1,0:T(8,128)(2,1)S(1)}, u32[]{:S(2)}, u32[]{:S(2)}) collective-permute-start(bf16[64,1024]{1,0:T(8,128)(2,1)S(1)} %collective-permute-done.15.refs_3_), channel_id=1, source_target_pairs={{0,1},{1,0},{2,3},{3,2},{4,5},{5,4},{6,7},{7,6},{8,9},{9,8},{10,11... | collective-permute-start | bytes 393224 | tf_op jit(solution)/shard_map/ppermute | solution.py:20
  65.8 1.7 %copy-start.3 = (f32[128]{0:T(128)}, f32[128]{0:T(128)S(1)}, u32[]{:S(2)}) copy-start(f32[128]{0:T(128)S(1)} %log_add_fusion) | copy-start | bytes 1540
where the time goes:
time: 67.7 us; the launch traced here: 67.5 us
  Pallas kernels  37.1 us (55%)
  starting transfers between devices  14.4 us (21%)
  blocking collectives  11.4 us (17%)
  other arithmetic  1.75 us (3%)
  waiting for transfers between devices  1.38 us (2%)
  between operations  0.85 us (1%)
  local copies, waits for them, and re-layouts  0.68 us (1%)
    pallas_call x6, Pallas kernels, stage(): pl.pallas_call(functools.partial(stage_kernel, plan), in_specs=specs, out...  37 us
    all_to_all x1, blocking collectives, local(): parts = lax.all_to_all(sent, ('rows', 'vocab'), 0, 0, tiled=True)  11.4 us
    ppermute x12, starting transfers between devices, swap(): return lax.ppermute(x, axis, [(i, i ^ distance) for i in range(size)])  6.74 us
    ppermute x3, starting transfers between devices, local(): lax.ppermute(up, 'rows', ahead)  3.69 us
    ppermute x3, starting transfers between devices, local(): lax.ppermute(down, 'rows', back)  2.44 us
    transpose x1, other arithmetic, local(): return (log_probs.T, lse.reshape(all_rows))  1.69 us
    ppermute x1, starting transfers between devices, local(): coming = [(j, lax.ppermute(up, 'rows', ahead))]  1.58 us
    ppermute x12, waiting for transfers between devices, swap(): return lax.ppermute(x, axis, [(i, i ^ distance) for i in range(size)])  1.36 us
  transfers between devices with their start and end apart: 19, of which 1 were waited for; matrix products, arithmetic and copies ran while one was open for 0% of the time, Pallas kernels for 50%

commit v1 on v0

--- a/solution.py
+++ b/solution.py
@@ -10,6 +10,7 @@
 lowest = -1e30
 reachable = -1e29
 slots = 4
+raw_slots = 5
 
 
 def ring_order(size):
@@ -23,6 +24,10 @@
 def row_tile(columns):
     fits = [t for t in range(16, 529, 16) if columns % t == 0]
     return max(fits) if fits else columns
+
+
+def up_to(size, step):
+    return -(-size // step) * step
 
 
 def ring_place(offset, count):
@@ -35,6 +40,7 @@
 
 def stage_kernel(plan, *refs):
     rows_count, block, depth, columns, all_rows = plan["sizes"]
+    half = plan["vocab_count"] // 2
     refs = list(refs)
     take = lambda n: [refs.pop(0) for _ in range(n)]
     (weight,) = take(1)
@@ -43,15 +49,17 @@
     else:
         take(1)
     if plan["first"]:
-        states, table = take(plan["vocab_count"]), take(1)[0]
+        (rules_in,) = take(1)
     elif plan["compute"]:
         take(1)
     chunks = [(slot, take(2)) for slot in plan["compute"]]
     (held,) = take(1)
     acc = take(1)[0] if plan["compute"] else None
     lse = take(1)[0] if plan["last"] else None
-    table_out = take(1)[0] if plan["load_table"] else None
-    hidden, turned, marks, sems = take(4)
+    if plan["compute"]:
+        hidden, turned, marks, sems = take(4)
+    else:
+        rules_out, raw, raw_sems, sems = take(4)
 
     tile = row_tile(columns)
     tiles = columns // tile
@@ -61,37 +69,50 @@
         for t in range(tiles):
             span = pl.ds(t * tile, tile)
             copies.append((weight.at[span, pl.ds(at, depth)], held.at[slot, span, :]))
-    if plan["load_table"]:
+    copies = [pltpu.make_async_copy(a, b, sems.at[n]) for n, (a, b) in enumerate(copies)]
+    if plan["compute"]:
+        for copy in copies:
+            copy.start()
+    else:
+        raw_copies = []
         for t in range(tiles):
             span = pl.ds(t * tile, tile)
-            copies.append((table_in.at[span, :], table_out.at[span, :]))
-    copies = [pltpu.make_async_copy(a, b, sems.at[n]) for n, (a, b) in enumerate(copies)]
-    for copy in copies:
-        copy.start()
+            raw_copies.append(pltpu.make_async_copy(table_in.at[span, :], raw.at[t % raw_slots], raw_sems.at[t]))
+        for copy in raw_copies[:raw_slots]:
+            copy.start()
+        for t in range(tiles):
+            raw_copies[t].wait()
+            copies[t].start()
+            rules_out[pl.ds(t * tile, tile), :] = raw[t % raw_slots].astype(jnp.float32).astype(jnp.bfloat16)
+            if t + raw_slots < tiles:
+                raw_copies[t + raw_slots].start()
 
     if plan["compute"]:
         vocab_at = lax.axis_index("vocab")
         for c, (_, pieces) in enumerate(chunks):
             for other, ref in enumerate(pieces):
-                for j in range(ref.shape[0] // block):
+                for j in range(half):
                     owner = vocab_at ^ (2 * j + other)
                     at = pl.multiple_of(owner * block, block)
                     hidden[pl.ds(at, block), :] = ref[j * block : (j + 1) * block, :]
             turned[c] = hidden[...].astype(jnp.float32).T.astype(jnp.bfloat16)
         if plan["first"]:
-            state_count = table.shape[1]
-            state = lax.broadcasted_iota(jnp.int32, (state_count, all_rows), 0)
+            state_count = rules_in.shape[1]
             owner = lax.broadcasted_iota(jnp.int32, (1, all_rows), 1) // block
-            wanted = jnp.zeros((1, all_rows), jnp.int32)
-            for d, part in enumerate(states):
-                wanted = jnp.where(owner == (vocab_at ^ d), jnp.tile(part[...], (1, all_rows // block)), wanted)
+            wanted = jnp.zeros((1, all_rows), jnp.float32)
+            for other, ref in enumerate(chunks[0][1]):
+                digits = ref[half * block :, : up_to(half * block, 128)].astype(jnp.float32)
+                states = digits[0:1] * 256.0 + digits[1:2]
+                for j in range(half):
+                    part = jnp.tile(states[:, j * block : (j + 1) * block], (1, all_rows // block))
+                    wanted = jnp.where(owner == (vocab_at ^ (2 * j + other)), part, wanted)
+            state = lax.broadcasted_iota(jnp.int32, (state_count, all_rows), 0).astype(jnp.float32)
             marks[...] = (state == wanted).astype(jnp.float32).astype(jnp.bfloat16)
 
         def work(t, carry):
             span = pl.ds(pl.multiple_of(t * tile, tile), tile) if tiles > 1 else slice(None)
             if plan["first"]:
-                rules = table[span, :].astype(jnp.float32).astype(jnp.bfloat16)
-                allowed = jnp.dot(rules, marks[...], preferred_element_type=jnp.float32) > 0.5
+                allowed = jnp.dot(rules_in[span, :], marks[...], preferred_element_type=jnp.float32) > 0.5
                 total = jnp.where(allowed, 0.0, lowest)
             else:
                 total = acc[span, :]
@@ -118,22 +139,22 @@
         copy.wait()
 
 
-def stage(plan, weight, table_in, states, table, held, acc, chunks):
+def stage(plan, weight, table, rules, held, acc, chunks):
     rows_count, block, depth, columns, all_rows = plan["sizes"]
     vmem = pl.BlockSpec(memory_space=pltpu.VMEM)
     keep = lambda x: pltpu.with_memory_space_constraint(x, pltpu.VMEM)
     args, specs, out, alias = [weight], [pl.BlockSpec(memory_space=pl.ANY)], [], {}
-    state_count = table_in.shape[1]
+    state_count = table.shape[1]
     if plan["load_table"]:
-        args.append(pltpu.with_memory_space_constraint(table_in, pltpu.HBM))
+        args.append(pltpu.with_memory_space_constraint(table, pltpu.HBM))
         specs.append(pl.BlockSpec(memory_space=pltpu.HBM))
     else:
         alias[len(args)] = 0
         args.append(keep(held))
         specs.append(vmem)
     if plan["first"]:
-        args += [*states, keep(table)]
-        specs += [vmem] * (len(states) + 1)
+        args.append(keep(rules))
+        specs.append(vmem)
     elif plan["compute"]:
         alias[len(args)] = 1
         args.append(keep(acc))
@@ -145,9 +166,23 @@
         out.append(pltpu.VMEM((columns, all_rows), jnp.float32))
     if plan["last"]:
         out.append(jax.ShapeDtypeStruct((1, all_rows), jnp.float32))
-    if plan["load_table"]:
-        out.append(pltpu.VMEM((columns, state_count), jnp.int32))
-    tiles = columns // row_tile(columns)
+    tile = row_tile(columns)
+    tiles = columns // tile
+    sems = pltpu.SemaphoreType.DMA((max(1, tiles * len(plan["load"])),))
+    if plan["compute"]:
+        scratch = [
+            pltpu.VMEM((all_rows, depth), jnp.bfloat16),
+            pltpu.VMEM((len(plan["compute"]), depth, all_rows), jnp.bfloat16),
+            pltpu.VMEM((state_count, all_rows), jnp.bfloat16),
+            sems,
+        ]
+    else:
+        out.append(pltpu.VMEM((columns, state_count), jnp.bfloat16))
+        scratch = [
+            pltpu.VMEM((raw_slots, tile, state_count), jnp.int32),
+            pltpu.SemaphoreType.DMA((tiles,)),
+            sems,
+        ]
     moved = 2 * columns * depth * len(plan["load"]) + 4 * columns * state_count * plan["load_table"]
     return pl.pallas_call(
         functools.partial(stage_kernel, plan),
@@ -155,13 +190,8 @@
         out_shape=out,
         out_specs=[vmem] * len(out),
         input_output_aliases=alias,
-        scratch_shapes=[
-            pltpu.VMEM((all_rows, depth), jnp.bfloat16),
-            pltpu.VMEM((max(1, len(plan["compute"])), depth, all_rows), jnp.bfloat16),
-            pltpu.VMEM((state_count, all_rows), jnp.bfloat16),
-            pltpu.SemaphoreType.DMA((max(1, tiles * (len(plan["load"]) + plan["load_table"])),)),
-        ],
-        compiler_params=pltpu.CompilerParams(vmem_limit_bytes=5 * 2**20),
+        scratch_shapes=scratch,
+        compiler_params=pltpu.CompilerParams(vmem_limit_bytes=7 * 2**20),
         cost_estimate=pl.CostEstimate(
             flops=2 * all_rows * depth * columns * len(plan["compute"]),
             bytes_accessed=moved,
@@ -170,21 +200,36 @@
     )(*args)
 
 
-def join_kernel(*refs):
-    size = refs[0].shape[0]
-    for i, ref in enumerate(refs[:-1]):
-        refs[-1][i * size : (i + 1) * size, :] = ref[...]
-
-
-def join(parts):
-    rows, width = parts[0].shape
+def join_kernel(half, *refs):
+    pieces, states, (plain, marked) = refs[:half], refs[half : 2 * half], refs[2 * half :]
+    block = pieces[0].shape[0]
+    for j, ref in enumerate(pieces):
+        plain[j * block : (j + 1) * block, :] = ref[...]
+        marked[j * block : (j + 1) * block, :] = ref[...]
+    width = up_to(half * block, 128)
+    owner = lax.broadcasted_iota(jnp.int32, (1, width), 1) // block
+    joined = jnp.zeros((1, width), jnp.int32)
+    for j, ref in enumerate(states):
+        joined = jnp.where(owner == j, jnp.tile(ref[...], (1, width // block)), joined)
+    digit = lax.broadcasted_iota(jnp.int32, (16, width), 0)
+    digits = jnp.where(digit == 0, joined // 256, jnp.where(digit == 1, joined % 256, 0))
+    marked[half * block :, :width] = digits.astype(jnp.float32).astype(jnp.bfloat16)
+
+
+def join(pieces, states):
+    block, depth = pieces[0].shape
+    rows = block * len(pieces)
+    vmem = pl.BlockSpec(memory_space=pltpu.VMEM)
     return pl.pallas_call(
-        join_kernel,
-        in_specs=[pl.BlockSpec(memory_space=pltpu.VMEM)] * len(parts),
-        out_specs=pl.BlockSpec(memory_space=pltpu.VMEM),
-        out_shape=jax.ShapeDtypeStruct((rows * len(parts), width), parts[0].dtype),
-        compiler_params=pltpu.CompilerParams(vmem_limit_bytes=2 * 2**20),
-    )(*parts)
+        functools.partial(join_kernel, len(pieces)),
+        in_specs=[vmem] * (2 * len(pieces)),
+        out_specs=[vmem] * 2,
+        out_shape=[
+            jax.ShapeDtypeStruct((rows, depth), jnp.bfloat16),
+            jax.ShapeDtypeStruct((rows + 16, depth), jnp.bfloat16),
+        ],
+        compiler_params=pltpu.CompilerParams(vmem_limit_bytes=4 * 2**20),
+    )(*pieces, *states)
 
 
 def local(rows_count, vocab_count, hidden_rows, row_states, head_weight, grammar_table):
@@ -192,11 +237,11 @@
     columns = head_weight.shape[1]
     half = vocab_count // 2
     all_rows = block * vocab_count
-    weight, table_in = head_weight.T, grammar_table.T
+    weight, table = head_weight.T, grammar_table.T
 
     row_states = row_states.reshape(1, block)
-    states = [row_states] + [swap(row_states, "vocab", vocab_count, d) for d in range(1, vocab_count)]
-    own = [hidden_rows] + [swap(hidden_rows, "vocab", vocab_count, 2 * d) for d in range(1, half)]
+    shared = lambda x: [x] + [swap(x, "vocab", vocab_count, 2 * d) for d in range(1, half)]
+    pieces, states = shared(hidden_rows), shared(row_states)
     plan = dict(
         vocab_count=vocab_count,
         sizes=(rows_count, block, depth, columns, all_rows),
@@ -206,16 +251,16 @@
         first=False,
         last=False,
     )
-    held, table = stage(plan, weight, table_in, states, None, None, None, [])
-    own, states, held, table = lax.optimization_barrier((own, states, held, table))
-    own = join(own)
+    held, rules = stage(plan, weight, table, None, None, None, [])
+    pieces, states, held, rules = lax.optimization_barrier((pieces, states, held, rules))
+    own, marked = join(pieces, states)
 
     order = ring_order(rows_count)
     ahead = [(order[i], order[(i + 1) % rows_count]) for i in range(rows_count)]
     back = [(b, a) for a, b in ahead]
     last_hop = rows_count // 2
     acc, load, used = None, plan["load"], 1
-    arrived = [(0, own)]
+    arrived = [(0, marked)]
     up = down = own
     for j in range(1, last_hop + 2):
         coming = []
@@ -236,7 +281,7 @@
             first=j == 1,
             last=j > last_hop,
         )
-        res = list(stage(plan, weight, table_in, states, table, held, acc, chunks))
+        res = list(stage(plan, weight, table, rules, held, acc, chunks))
         held, acc = res[:2]
         if plan["last"]:
             lse = res[2]

time: 67.7 us -> 65.9 us (0.973)
  starting transfers between devices: 14.4 us -> 13.1 us
  blocking collectives: 11.4 us -> 12.3 us
    ppermute x12 -> x10, starting transfers between devices: 6.74 us -> 4.96 us  [swap(): return lax.ppermute(x, axis, [(i, i ^ distance) for i in range(size)])]
    all_to_all x1, blocking collectives: 11.4 us -> 12.3 us  [local(): parts = lax.all_to_all(sent, ('rows', 'vocab'), 0, 0, tiled=True)]
    pallas_call x6, Pallas kernels: 37 us -> 36.4 us  [stage(): pl.pallas_call(functools.partial(stage_kernel, plan), in_specs=specs, out...]
    ppermute x12 -> x10, waiting for transfers between devices: 1.36 us -> 1.36 us  [swap(): return lax.ppermute(x, axis, [(i, i ^ distance) for i in range(size)])]
  transfers between devices with their start and end apart: 19 -> 17, of which waited for: 1 -> 1; matrix products, arithmetic and copies ran while one was open for 0% -> 0% of each run, Pallas kernels for 50% -> 50%
where the time goes in v1:
time: 65.9 us; the launch traced here: 65.8 us
  Pallas kernels  36.5 us (55%)
  starting transfers between devices  13.1 us (20%)
  blocking collectives  12.3 us (19%)
  other arithmetic  1.75 us (3%)
  waiting for transfers between devices  1.38 us (2%)
  between operations  0.83 us (1%)
    pallas_call x6, Pallas kernels, stage(): pl.pallas_call(functools.partial(stage_kernel, plan), in_specs=specs, out...  36.4 us
    all_to_all x1, blocking collectives, local(): parts = lax.all_to_all(sent, ('rows', 'vocab'), 0, 0, tiled=True)  12.3 us
    ppermute x10, starting transfers between devices, swap(): return lax.ppermute(x, axis, [(i, i ^ distance) for i in range(size)])  4.96 us
    ppermute x3, starting transfers between devices, local(): lax.ppermute(up, 'rows', ahead)  4.17 us
    ppermute x1, starting transfers between devices, local(): coming = [(j, lax.ppermute(up, 'rows', ahead))]  2 us
    ppermute x3, starting transfers between devices, local(): lax.ppermute(down, 'rows', back)  1.96 us
    transpose x1, other arithmetic, local(): return (log_probs.T, lse.reshape(all_rows))  1.69 us
    ppermute x10, waiting for transfers between devices, swap(): return lax.ppermute(x, axis, [(i, i ^ distance) for i in range(size)])  1.36 us
  transfers between devices with their start and end apart: 17, of which 1 were waited for; matrix products, arithmetic and copies ran while one was open for 0% of the time, Pallas kernels for 50%

profile of v1, /device:TPU:0, one launch (start us, length us, event | category | flops | bytes accessed | tf_op | source)
XLA Modules:
  0.0 65.8 jit_solution(9424500629784325280)
XLA Ops:
  0.6 3.0 %collective-permute-start = (bf16[32,1024]{1,0:T(8,128)(2,1)}, bf16[32,1024]{1,0:T(8,128)(2,1)S(1)}, u32[]{:S(2)}, u32[]{:S(2)}) collective-permute-start(bf16[32,1024]{1,0:T(8,128)(2,1)} %refs_0_), channel_id=1, source_target_pairs={{0,2},{1,3},{2,0},{3,1},{4,6},{5,7},{6,4},{7,5},{8,10},{9,11},{10,... | collective-permute-start | bytes 196616 | tf_op jit(solution)/shard_map/ppermute | solution.py:21
  3.7 0.1 collective-permute-start.1
  3.7 0.0 copy-start
  3.7 7.0 %shard_map.59 = (bf16[4,4752,1024]{2,1,0:T(8,128)(2,1)S(1)}, bf16[4752,512]{1,0:T(8,128)(2,1)S(1)}) custom-call(bf16[4752,8192]{1,0:T(8,128)(2,1)} %bitcast.refs_0_, s32[4752,512]{1,0:T(8,128)} %bitcast.10), custom_call_target="tpu_custom_call" | custom-call | bytes 19464192 | tf_op jit(solution)/shard_map/pallas_call | solution.py:187
  10.8 0.0 collective-permute-done.1.refs_3_
  10.8 0.0 collective-permute-done.refs_1_
  10.8 0.0 copy-done
  10.8 0.0 copy-done.1
  10.8 0.1 shard_map.60
  10.9 0.1 collective-permute-start.4
  11.0 2.1 %collective-permute-start.2 = (bf16[64,1024]{1,0:T(8,128)(2,1)S(1)}, bf16[64,1024]{1,0:T(8,128)(2,1)S(1)}, u32[]{:S(2)}, u32[]{:S(2)}) collective-permute-start(bf16[64,1024]{1,0:T(8,128)(2,1)S(1)} %get-tuple-element.43), channel_id=1, source_target_pairs={{0,8},{8,16},{16,24},{24,28},{28,20},{20,12},{12,4},{4,0},{1,9},{9... | collective-permute-start | bytes 393224 | tf_op jit(solution)/shard_map/ppermute | solution.py:268
  13.0 0.0 collective-permute-start.3
  13.1 0.0 collective-permute-done.4.refs_4_
  13.1 6.8 %shard_map.61 = (bf16[4,4752,1024]{2,1,0:T(8,128)(2,1)S(1)}, f32[4752,128]{1,0:T(8,128)S(1)}) custom-call(bf16[4752,8192]{1,0:T(8,128)(2,1)} %bitcast.refs_0_, bf16[4,4752,1024]{2,1,0:T(8,128)(2,1)S(1)} %get-tuple-element.44.refs_1_, bf16[4752,512]{1,0:T(8,128)(2,1)S(1)} %get-tuple-element.45.refs_2_, ...), custom_call_target="tpu_custom_call", output_to_operand_aliasing={{0}: (1, {})} | custom-call | flops 1245708288 | bytes 19464192 | tf_op jit(solution)/shard_map/pallas_call | solution.py:187
  19.9 0.0 collective-permute-done.2.refs_3_
  19.9 0.0 collective-permute-done.3.refs_5_
  19.9 0.2 collective-permute-start.7
  20.1 0.4 collective-permute-start.8
  20.5 2.0 %collective-permute-start.5 = (bf16[64,1024]{1,0:T(8,128)(2,1)S(1)}, bf16[64,1024]{1,0:T(8,128)(2,1)S(1)}, u32[]{:S(2)}, u32[]{:S(2)}) collective-permute-start(bf16[64,1024]{1,0:T(8,128)(2,1)S(1)} %collective-permute-done.2.refs_3_), channel_id=1, source_target_pairs={{0,8},{8,16},{16,24},{24,28},{28,20},{20,12},{12,4},{4,0},{1,9},{9... | collective-permute-start | bytes 393224 | tf_op jit(solution)/shard_map/ppermute | solution.py:268
  22.5 0.0 collective-permute-start.6
  22.5 0.0 collective-permute-done.7.refs_4_
  22.5 0.0 collective-permute-done.8.refs_6_
  22.5 6.9 %shard_map.62 = (bf16[4,4752,1024]{2,1,0:T(8,128)(2,1)S(1)}, f32[4752,128]{1,0:T(8,128)S(1)}) custom-call(bf16[4752,8192]{1,0:T(8,128)(2,1)} %bitcast.refs_0_, bf16[4,4752,1024]{2,1,0:T(8,128)(2,1)S(1)} %get-tuple-element.51.refs_1_, f32[4752,128]{1,0:T(8,128)S(1)} %get-tuple-element.52.refs_2_, ...), custom_call_target="tpu_custom_call", output_to_operand_aliasing={{0}: (1, {}), {1}: (2, {})} | custom-call | flops 2491416576 | bytes 19464192 | tf_op jit(solution)/shard_map/pallas_call | solution.py:187
  29.4 0.0 collective-permute-done.5.refs_3_
  29.4 0.0 collective-permute-done.6.refs_5_
  29.4 0.1 collective-permute-start.11
  29.5 0.5 collective-permute-start.12
  30.0 1.9 %collective-permute-start.10 = (bf16[64,1024]{1,0:T(8,128)(2,1)S(1)}, bf16[64,1024]{1,0:T(8,128)(2,1)S(1)}, u32[]{:S(2)}, u32[]{:S(2)}) collective-permute-start(bf16[64,1024]{1,0:T(8,128)(2,1)S(1)} %collective-permute-done.6.refs_5_), channel_id=1, source_target_pairs={{8,0},{16,8},{24,16},{28,24},{20,28},{12,20},{4,12},{0,4},{9,1},{1... | collective-permute-start | bytes 393224 | tf_op jit(solution)/shard_map/ppermute | solution.py:268
  31.9 0.1 collective-permute-start.9
  32.0 0.0 collective-permute-done.11.refs_4_
  32.0 0.0 collective-permute-done.12.refs_6_
  32.1 6.9 %shard_map.63 = (bf16[4,4752,1024]{2,1,0:T(8,128)(2,1)S(1)}, f32[4752,128]{1,0:T(8,128)S(1)}) custom-call(bf16[4752,8192]{1,0:T(8,128)(2,1)} %bitcast.refs_0_, bf16[4,4752,1024]{2,1,0:T(8,128)(2,1)S(1)} %get-tuple-element.57.refs_1_, f32[4752,128]{1,0:T(8,128)S(1)} %get-tuple-element.58.refs_2_, ...), custom_call_target="tpu_custom_call", output_to_operand_aliasing={{0}: (1, {}), {1}: (2, {})} | custom-call | flops 2491416576 | bytes 19464192 | tf_op jit(solution)/shard_map/pallas_call | solution.py:187
  38.9 0.0 collective-permute-done.10.refs_5_
  38.9 0.0 collective-permute-done.9.refs_3_
  38.9 0.1 collective-permute-start.14
  39.0 0.5 collective-permute-start.15
  39.5 2.0 %collective-permute-start.13 = (bf16[64,1024]{1,0:T(8,128)(2,1)S(1)}, bf16[64,1024]{1,0:T(8,128)(2,1)S(1)}, u32[]{:S(2)}, u32[]{:S(2)}) collective-permute-start(bf16[64,1024]{1,0:T(8,128)(2,1)S(1)} %collective-permute-done.9.refs_3_), channel_id=1, source_target_pairs={{0,8},{8,16},{16,24},{24,28},{28,20},{20,12},{12,4},{4,0},{1,9},{9... | collective-permute-start | bytes 393224 | tf_op jit(solution)/shard_map/ppermute | solution.py:270
  41.5 0.0 collective-permute-done.14.refs_4_
  41.5 0.0 collective-permute-done.15.refs_6_
  41.5 5.5 %shard_map.64 = (bf16[4,4752,1024]{2,1,0:T(8,128)(2,1)S(1)}, f32[4752,128]{1,0:T(8,128)S(1)}) custom-call(bf16[4752,8192]{1,0:T(8,128)(2,1)} %bitcast.refs_0_, bf16[4,4752,1024]{2,1,0:T(8,128)(2,1)S(1)} %get-tuple-element.62.refs_1_, f32[4752,128]{1,0:T(8,128)S(1)} %get-tuple-element.63.refs_2_, ...), custom_call_target="tpu_custom_call", output_to_operand_aliasing={{0}: (1, {}), {1}: (2, {})} | custom-call | flops 2491416576 | bytes 9732096 | tf_op jit(solution)/shard_map/pallas_call | solution.py:187
  47.0 0.0 collective-permute-done.13.refs_3_
  47.0 0.1 collective-permute-start.16
  47.1 1.3 %collective-permute-done.16.refs_4_ = bf16[64,1024]{1,0:T(8,128)(2,1)S(1)} collective-permute-done((bf16[64,1024]{1,0:T(8,128)(2,1)S(1)}, bf16[64,1024]{1,0:T(8,128)(2,1)S(1)}, u32[]{:S(2)}, u32[]{:S(2)}) %collective-permute-start.16) | collective-permute-done | bytes 131104 | tf_op jit(solution)/shard_map/ppermute | solution.py:21
  48.4 3.3 %shard_map.65 = (bf16[4,4752,1024]{2,1,0:T(8,128)(2,1)S(1)}, f32[4752,128]{1,0:T(8,128)S(1)}, f32[1,128]{1,0:T(1,128)S(1)}) custom-call(bf16[4752,8192]{1,0:T(8,128)(2,1)} %bitcast.refs_0_, bf16[4,4752,1024]{2,1,0:T(8,128)(2,1)S(1)} %get-tuple-element.67.refs_1_, ...), custom_call_target="tpu_custom_call", output_to_operand_aliasing={{0}: (1, {}), {1}: (2, {})} | custom-call | flops 1245708288 | tf_op jit(solution)/shard_map/pallas_call | solution.py:187
  51.8 12.3 %all_to_all.5 = f32[32,1,128]{2,1,0:T(1,128)S(1)} all-to-all(f32[32,1,128]{2,1,0:T(1,128)S(1)} %broadcast_in_dim.14), channel_id=1, replica_groups=mesh['rows'=8,'vocab'=4] {'rows','vocab'}, dimensions={0} | all-to-all | bytes 32768 | tf_op jit(solution)/shard_map/all_to_all | solution.py:295
  64.1 0.0 copy-start.2
  64.1 1.7 %select_bitcast_fusion = f32[128,4752]{0,1:T(8,128)} fusion(f32[4752,128]{1,0:T(8,128)S(1)} %get-tuple-element.70, f32[128]{0:T(128)S(1)} %log_add_fusion), kind=kLoop, calls=%fused_computation | loop fusion | flops 1824768 | bytes 4866560 | tf_op jit(solution)/shard_map/transpose | solution.py:299
  65.8 0.0 copy-done.2
  (5 shorter events, 0.1 us)
Async XLA Ops:
  0.6 10.2 %collective-permute-start = (bf16[32,1024]{1,0:T(8,128)(2,1)}, bf16[32,1024]{1,0:T(8,128)(2,1)S(1)}, u32[]{:S(2)}, u32[]{:S(2)}) collective-permute-start(bf16[32,1024]{1,0:T(8,128)(2,1)} %refs_0_), channel_id=1, source_target_pairs={{0,2},{1,3},{2,0},{3,1},{4,6},{5,7},{6,4},{7,5},{8,10},{9,11},{10,... | collective-permute-start | bytes 196616 | tf_op jit(solution)/shard_map/ppermute | solution.py:21
  3.7 7.1 %collective-permute-start.1 = (s32[1,32]{1,0:T(1,128)}, s32[1,32]{1,0:T(1,128)S(1)}, u32[]{:S(2)}, u32[]{:S(2)}) collective-permute-start(s32[1,32]{1,0:T(1,128)} %bitcast.7), channel_id=1, source_target_pairs={{0,2},{1,3},{2,0},{3,1},{4,6},{5,7},{6,4},{7,5},{8,10},{9,11},{10,... | collective-permute-start | bytes 392 | tf_op jit(solution)/shard_map/ppermute | solution.py:21
  3.7 7.0 %copy-start = (bf16[32,1024]{1,0:T(8,128)(2,1)S(1)}, bf16[32,1024]{1,0:T(8,128)(2,1)}, u32[]{:S(2)}) copy-start(bf16[32,1024]{1,0:T(8,128)(2,1)} %refs_0_) | copy-start | bytes 196612
  3.7 7.1 %copy-start.1 = (s32[32]{0:T(128)S(1)}, s32[32]{0:T(128)}, u32[]{:S(2)}) copy-start(s32[32]{0:T(128)} %param.5) | copy-start | bytes 388
  10.9 2.2 %collective-permute-start.4 = (bf16[80,1024]{1,0:T(8,128)(2,1)S(1)}, bf16[80,1024]{1,0:T(8,128)(2,1)S(1)}, u32[]{:S(2)}, u32[]{:S(2)}) collective-permute-start(bf16[80,1024]{1,0:T(8,128)(2,1)S(1)} %get-tuple-element.46.refs_3_), channel_id=1, source_target_pairs={{0,1},{1,0},{2,3},{3,2},{4,5},{5,4},{6,7},{7,6},{8,9},{9,8},{10,11... | collective-permute-start | bytes 491528 | tf_op jit(solution)/shard_map/ppermute | solution.py:21
  11.0 8.9 %collective-permute-start.2 = (bf16[64,1024]{1,0:T(8,128)(2,1)S(1)}, bf16[64,1024]{1,0:T(8,128)(2,1)S(1)}, u32[]{:S(2)}, u32[]{:S(2)}) collective-permute-start(bf16[64,1024]{1,0:T(8,128)(2,1)S(1)} %get-tuple-element.43), channel_id=1, source_target_pairs={{0,8},{8,16},{16,24},{24,28},{28,20},{20,12},{12,4},{4,0},{1,9},{9... | collective-permute-start | bytes 393224 | tf_op jit(solution)/shard_map/ppermute | solution.py:268
  13.0 6.9 %collective-permute-start.3 = (bf16[64,1024]{1,0:T(8,128)(2,1)S(1)}, bf16[64,1024]{1,0:T(8,128)(2,1)S(1)}, u32[]{:S(2)}, u32[]{:S(2)}) collective-permute-start(bf16[64,1024]{1,0:T(8,128)(2,1)S(1)} %get-tuple-element.43), channel_id=1, source_target_pairs={{8,0},{16,8},{24,16},{28,24},{20,28},{12,20},{4,12},{0,4},{9,1},{1... | collective-permute-start | bytes 393224 | tf_op jit(solution)/shard_map/ppermute | solution.py:268
  19.9 2.6 %collective-permute-start.7 = (bf16[64,1024]{1,0:T(8,128)(2,1)S(1)}, bf16[64,1024]{1,0:T(8,128)(2,1)S(1)}, u32[]{:S(2)}, u32[]{:S(2)}) collective-permute-start(bf16[64,1024]{1,0:T(8,128)(2,1)S(1)} %collective-permute-done.2.refs_3_), channel_id=1, source_target_pairs={{0,1},{1,0},{2,3},{3,2},{4,5},{5,4},{6,7},{7,6},{8,9},{9,8},{10,11... | collective-permute-start | bytes 393224 | tf_op jit(solution)/shard_map/ppermute | solution.py:21
  20.1 2.4 %collective-permute-start.8 = (bf16[64,1024]{1,0:T(8,128)(2,1)S(1)}, bf16[64,1024]{1,0:T(8,128)(2,1)S(1)}, u32[]{:S(2)}, u32[]{:S(2)}) collective-permute-start(bf16[64,1024]{1,0:T(8,128)(2,1)S(1)} %collective-permute-done.3.refs_5_), channel_id=1, source_target_pairs={{0,1},{1,0},{2,3},{3,2},{4,5},{5,4},{6,7},{7,6},{8,9},{9,8},{10,11... | collective-permute-start | bytes 393224 | tf_op jit(solution)/shard_map/ppermute | solution.py:21
  20.5 8.9 %collective-permute-start.5 = (bf16[64,1024]{1,0:T(8,128)(2,1)S(1)}, bf16[64,1024]{1,0:T(8,128)(2,1)S(1)}, u32[]{:S(2)}, u32[]{:S(2)}) collective-permute-start(bf16[64,1024]{1,0:T(8,128)(2,1)S(1)} %collective-permute-done.2.refs_3_), channel_id=1, source_target_pairs={{0,8},{8,16},{16,24},{24,28},{28,20},{20,12},{12,4},{4,0},{1,9},{9... | collective-permute-start | bytes 393224 | tf_op jit(solution)/shard_map/ppermute | solution.py:268
  22.5 6.9 %collective-permute-start.6 = (bf16[64,1024]{1,0:T(8,128)(2,1)S(1)}, bf16[64,1024]{1,0:T(8,128)(2,1)S(1)}, u32[]{:S(2)}, u32[]{:S(2)}) collective-permute-start(bf16[64,1024]{1,0:T(8,128)(2,1)S(1)} %collective-permute-done.3.refs_5_), channel_id=1, source_target_pairs={{8,0},{16,8},{24,16},{28,24},{20,28},{12,20},{4,12},{0,4},{9,1},{1... | collective-permute-start | bytes 393224 | tf_op jit(solution)/shard_map/ppermute | solution.py:268
  29.4 2.6 %collective-permute-start.11 = (bf16[64,1024]{1,0:T(8,128)(2,1)S(1)}, bf16[64,1024]{1,0:T(8,128)(2,1)S(1)}, u32[]{:S(2)}, u32[]{:S(2)}) collective-permute-start(bf16[64,1024]{1,0:T(8,128)(2,1)S(1)} %collective-permute-done.5.refs_3_), channel_id=1, source_target_pairs={{0,1},{1,0},{2,3},{3,2},{4,5},{5,4},{6,7},{7,6},{8,9},{9,8},{10,11... | collective-permute-start | bytes 393224 | tf_op jit(solution)/shard_map/ppermute | solution.py:21
  29.5 2.5 %collective-permute-start.12 = (bf16[64,1024]{1,0:T(8,128)(2,1)S(1)}, bf16[64,1024]{1,0:T(8,128)(2,1)S(1)}, u32[]{:S(2)}, u32[]{:S(2)}) collective-permute-start(bf16[64,1024]{1,0:T(8,128)(2,1)S(1)} %collective-permute-done.6.refs_5_), channel_id=1, source_target_pairs={{0,1},{1,0},{2,3},{3,2},{4,5},{5,4},{6,7},{7,6},{8,9},{9,8},{10,11... | collective-permute-start | bytes 393224 | tf_op jit(solution)/shard_map/ppermute | solution.py:21
  30.0 8.9 %collective-permute-start.10 = (bf16[64,1024]{1,0:T(8,128)(2,1)S(1)}, bf16[64,1024]{1,0:T(8,128)(2,1)S(1)}, u32[]{:S(2)}, u32[]{:S(2)}) collective-permute-start(bf16[64,1024]{1,0:T(8,128)(2,1)S(1)} %collective-permute-done.6.refs_5_), channel_id=1, source_target_pairs={{8,0},{16,8},{24,16},{28,24},{20,28},{12,20},{4,12},{0,4},{9,1},{1... | collective-permute-start | bytes 393224 | tf_op jit(solution)/shard_map/ppermute | solution.py:268
  31.9 7.0 %collective-permute-start.9 = (bf16[64,1024]{1,0:T(8,128)(2,1)S(1)}, bf16[64,1024]{1,0:T(8,128)(2,1)S(1)}, u32[]{:S(2)}, u32[]{:S(2)}) collective-permute-start(bf16[64,1024]{1,0:T(8,128)(2,1)S(1)} %collective-permute-done.5.refs_3_), channel_id=1, source_target_pairs={{0,8},{8,16},{16,24},{24,28},{28,20},{20,12},{12,4},{4,0},{1,9},{9... | collective-permute-start | bytes 393224 | tf_op jit(solution)/shard_map/ppermute | solution.py:268
  38.9 2.6 %collective-permute-start.14 = (bf16[64,1024]{1,0:T(8,128)(2,1)S(1)}, bf16[64,1024]{1,0:T(8,128)(2,1)S(1)}, u32[]{:S(2)}, u32[]{:S(2)}) collective-permute-start(bf16[64,1024]{1,0:T(8,128)(2,1)S(1)} %collective-permute-done.9.refs_3_), channel_id=1, source_target_pairs={{0,1},{1,0},{2,3},{3,2},{4,5},{5,4},{6,7},{7,6},{8,9},{9,8},{10,11... | collective-permute-start | bytes 393224 | tf_op jit(solution)/shard_map/ppermute | solution.py:21
  39.0 2.5 %collective-permute-start.15 = (bf16[64,1024]{1,0:T(8,128)(2,1)S(1)}, bf16[64,1024]{1,0:T(8,128)(2,1)S(1)}, u32[]{:S(2)}, u32[]{:S(2)}) collective-permute-start(bf16[64,1024]{1,0:T(8,128)(2,1)S(1)} %collective-permute-done.10.refs_5_), channel_id=1, source_target_pairs={{0,1},{1,0},{2,3},{3,2},{4,5},{5,4},{6,7},{7,6},{8,9},{9,8},{10,11... | collective-permute-start | bytes 393224 | tf_op jit(solution)/shard_map/ppermute | solution.py:21
  39.5 7.5 %collective-permute-start.13 = (bf16[64,1024]{1,0:T(8,128)(2,1)S(1)}, bf16[64,1024]{1,0:T(8,128)(2,1)S(1)}, u32[]{:S(2)}, u32[]{:S(2)}) collective-permute-start(bf16[64,1024]{1,0:T(8,128)(2,1)S(1)} %collective-permute-done.9.refs_3_), channel_id=1, source_target_pairs={{0,8},{8,16},{16,24},{24,28},{28,20},{20,12},{12,4},{4,0},{1,9},{9... | collective-permute-start | bytes 393224 | tf_op jit(solution)/shard_map/ppermute | solution.py:270
  47.0 1.4 %collective-permute-start.16 = (bf16[64,1024]{1,0:T(8,128)(2,1)S(1)}, bf16[64,1024]{1,0:T(8,128)(2,1)S(1)}, u32[]{:S(2)}, u32[]{:S(2)}) collective-permute-start(bf16[64,1024]{1,0:T(8,128)(2,1)S(1)} %collective-permute-done.13.refs_3_), channel_id=1, source_target_pairs={{0,1},{1,0},{2,3},{3,2},{4,5},{5,4},{6,7},{7,6},{8,9},{9,8},{10,11... | collective-permute-start | bytes 393224 | tf_op jit(solution)/shard_map/ppermute | solution.py:21
  64.1 1.7 %copy-start.2 = (f32[128]{0:T(128)}, f32[128]{0:T(128)S(1)}, u32[]{:S(2)}) copy-start(f32[128]{0:T(128)S(1)} %log_add_fusion) | copy-start | bytes 1540
